TPU v7x, 256 devices: a whole 4x4x8 slice. The times are simulated.
256 devices in a mesh: dp: 32 (over x, y, core), sp: 8 (over z).
Axes of the slice: x: 4, y: 4, z: 8, core: 2. Of those that a mesh axis runs over, the one named last changes fastest.
Arguments:
- queries: bfloat16 [32768, 4096], P(('dp', 'sp')), may hold values from -45 to 45
- grad_out: bfloat16 [32768, 4096], P(('dp', 'sp')), may hold values from -6 to 6
- key_heads: bfloat16 [32768, 1024], P(('dp', 'sp')), may hold values from -21 to 21
- value_heads: bfloat16 [32768, 1024], P(('dp', 'sp')), may hold values from -6 to 6
- seq_start: int32 [32768], P(('dp', 'sp')), may hold values from 0 to 32640, as said below
Outputs:
- query_grad: bfloat16 [32768, 4096], P(('dp', 'sp'))
- key_grad: bfloat16 [32768, 1024], P(('dp', 'sp'))
- value_grad: bfloat16 [32768, 1024], P(('dp', 'sp'))
Inputs may be any that keep to these rules, and one draw needn't show every extreme that they name: seq_start[t] is the first token of the sequence that holds token t. Every sequence starts at a multiple of 128 and is a whole number of 128-token rows; the last 128 tokens form a sequence of their own; every other sequence but the one just before them holds 2048 to 3072 tokens; no sequence touches more than 4 consecutive blocks of 1024 tokens, and in every draw some sequence touches 4.
All inputs are finite; a program needn't handle non-finite values.
Results may differ from a plain program's by a relative error of at most 0.012.
Values may be sent and summed in bfloat16 or wider, within the bound.
No kernel may reach another device: no remote copies, remote signals or barrier semaphores. Data moves between devices by JAX's collectives and lax.ppermute only.
A program may use at most 64 MiB of HBM per device.

v0:
```python
import functools
import math

import jax
import jax.numpy as jnp
from jax import lax
from jax.experimental import pallas as pl
from jax.experimental.pallas import tpu as pltpu
from jax.sharding import PartitionSpec as P

HQ = 32
HK = 8
HD = 128
UNIT = 128
SPAN = 4
BLK = 1024
UNITS = BLK // UNIT
STEPS = ((2, 1, 0, -1), (-2, -3, 4, 3))
PAST = (SPAN - 1) * BLK
HEADS = HQ // HK
TILE = 256
LANES = HEADS * TILE
CHUNK = 512
ROWS = SPAN * BLK + CHUNK
SCALE = 1.0 / math.sqrt(HD)
SCALE2 = SCALE * math.log2(math.e)
FILL = -1e30
BF, F32 = jnp.bfloat16, jnp.float32


def dot(a, b, ca, cb):
    return lax.dot_general(a, b, (((ca,), (cb,)), ((), ())), preferred_element_type=F32)


def fold(tile, reduce):
    return reduce(tile.reshape(CHUNK // 8, 8, LANES), axis=0)


def attention_kernel(last, info_ref, *refs):
    pieces, blocks, refs = refs[:4], refs[4:8], refs[8:]
    if last:
        sums, refs = refs[:2], refs[2:]
    dq_refs, refs = refs[:4], refs[4:]
    outs, refs = (refs[:4], refs[4:]) if last else (refs[:2], refs[2:])
    kbuf, vbuf, ebuf, pbuf, mbuf, dkacc, dvacc, dqacc, qobuf, dqbuf, in_sem, out_sem, *wide = refs
    loads = [(piece, qobuf.at[m]) for m, piece in enumerate(pieces)]
    for at, block in enumerate(blocks):
        rows = pl.ds(at * BLK, BLK)
        loads.append((block.at[:, pl.ds(0, HD)], kbuf.at[rows, :]))
        loads.append((block.at[:, pl.ds(HD, HD)], vbuf.at[rows, :]))
    if last:
        loads += [(sums[0], dkacc), (sums[1], dvacc)]
    loads = [pltpu.make_async_copy(a, b, in_sem.at[n]) for n, (a, b) in enumerate(loads)]
    for copy in loads:
        copy.start()
    kbuf[SPAN * BLK :, :] = jnp.zeros((CHUNK, HD), BF)
    vbuf[SPAN * BLK :, :] = jnp.zeros((CHUNK, HD), BF)
    if not last:
        dkacc[...] = jnp.zeros_like(dkacc)
        dvacc[...] = jnp.zeros_like(dvacc)
    for copy in loads:
        copy.wait()
    lane = lax.broadcasted_iota(jnp.int32, (1, LANES), 1) & (TILE - 1)

    def tile_step(pair, _):
        entry = UNITS + 8 * last + 4 * pair
        place = [info_ref[entry + 2 * n] for n in range(2)]
        unit = [info_ref[entry + 2 * n + 1] for n in range(2)]
        side = lambda low: jnp.concatenate(
            [
                qobuf[place[n], :, low + h * HD : low + (h + 1) * HD]
                for h in range(HEADS)
                for n in range(2)
            ],
            axis=0,
        )
        q_t, o_t = side(0), side(HEADS * HD)
        begin = [info_ref[u] for u in unit]
        row = [PAST + u * UNIT for u in unit]
        first = jnp.minimum(begin[0], begin[1])
        starts = jnp.where(lane < UNIT, begin[0], begin[1])
        query_id = jnp.where(lane < UNIT, row[0] + lane, row[1] + lane - UNIT)
        same = begin[0] == begin[1]
        plain = jnp.where(same, (jnp.minimum(row[0], row[1]) - first) // CHUNK, 0)
        count = (jnp.maximum(row[0], row[1]) + UNIT - first + CHUNK - 1) // CHUNK

        def keys(i):
            return pl.ds(pl.multiple_of(first + i * CHUNK, UNIT), CHUNK)

        def slot(i):
            return pl.ds(pl.multiple_of(i * CHUNK, CHUNK), CHUNK)

        def forward(masked, i, carry):
            top, total, weighted = carry
            at = keys(i)
            s = dot(kbuf[at, :], q_t, 1, 1)
            if masked:
                key_id = first + i * CHUNK + lax.broadcasted_iota(jnp.int32, (CHUNK, LANES), 0)
                s = jnp.where((key_id <= query_id) & (key_id >= starts), s, FILL)
            slopes = dot(vbuf[at, :], o_t, 1, 1)
            new = jnp.maximum(top, jnp.max(fold(s, jnp.max), axis=0, keepdims=True) * SCALE2)
            e = jnp.exp2(s * SCALE2 - new)
            ebuf[slot(i), :] = e
            pbuf[slot(i), :] = slopes
            mbuf[pl.ds(i, 1), :] = new
            shrink = jnp.exp2(top - new)
            total = total * shrink + fold(e, jnp.sum)
            return new, total, weighted * shrink + fold(e * slopes, jnp.sum)

        zero = jnp.zeros((8, LANES), F32)
        carry = (jnp.full((1, LANES), FILL, F32), zero, zero)
        plainly = functools.partial(forward, False)
        twice = lambda i, c: plainly(2 * i + 1, plainly(2 * i, c))
        carry = lax.fori_loop(0, plain // 2, twice, carry)
        carry = lax.fori_loop(plain // 2 * 2, plain, plainly, carry)
        top, total, weighted = lax.fori_loop(
            plain, count, functools.partial(forward, True), carry
        )
        inverse = 1.0 / jnp.sum(total, axis=0, keepdims=True)
        row_dot = jnp.sum(weighted, axis=0, keepdims=True) * inverse
        dqacc[...] = jnp.zeros_like(dqacc)

        def grads(i, _):
            w = ebuf[slot(i), :] * (jnp.exp2(mbuf[pl.ds(i, 1), :] - top) * inverse)
            ds = (w * (pbuf[slot(i), :] - row_dot)).astype(BF)
            at = keys(i)
            dvacc[at, :] += dot(w.astype(BF), o_t, 1, 0)
            dkacc[at, :] += dot(ds, q_t, 1, 0)
            dqacc[...] += dot(kbuf[at, :], ds, 0, 0)
            return 0

        def two_grads(i, _):
            grads(2 * i, 0)
            return grads(2 * i + 1, 0)

        lax.fori_loop(0, count // 2, two_grads, 0)
        lax.fori_loop(count // 2 * 2, count, grads, 0)
        for h in range(HEADS):
            dq = (dqacc[:, h * TILE : (h + 1) * TILE].T * SCALE).astype(BF)
            for n in range(2):
                dqbuf[place[n], :, h * HD : (h + 1) * HD] = dq[n * UNIT : (n + 1) * UNIT]
        return 0

    lax.fori_loop(0, 2, tile_step, 0)
    stores = []

    def store(a, b):
        stores.append(pltpu.make_async_copy(a, b, out_sem.at[len(stores)]))
        stores[-1].start()

    for m, out in enumerate(dq_refs):
        store(dqbuf.at[m], out)
    if last:
        for at, (held, out) in enumerate(zip(wide, outs)):
            low = at * BLK
            held[:, :HD] = (dkacc[low : low + BLK, :] * SCALE).astype(out.dtype)
            held[:, HD:] = dvacc[low : low + BLK, :].astype(out.dtype)
            store(held, out)
    else:
        store(dkacc, outs[0])
        store(dvacc, outs[1])
    for copy in stores:
        copy.wait()


def attend(last, info, pieces, blocks, sums=()):
    hbm = pl.BlockSpec(memory_space=pl.ANY)
    shape = jax.ShapeDtypeStruct
    scratch = [
        pltpu.VMEM((ROWS, HD), BF),
        pltpu.VMEM((ROWS, HD), BF),
        pltpu.VMEM((ROWS, LANES), F32),
        pltpu.VMEM((ROWS, LANES), F32),
        pltpu.VMEM((16, LANES), F32),
        pltpu.VMEM((ROWS, HD), F32),
        pltpu.VMEM((ROWS, HD), F32),
        pltpu.VMEM((HD, LANES), F32),
        pltpu.VMEM((4, UNIT, 2 * HEADS * HD), BF),
        pltpu.VMEM((4, UNIT, HEADS * HD), BF),
        pltpu.SemaphoreType.DMA((14,)),
        pltpu.SemaphoreType.DMA((8,)),
    ]
    if last:
        wide = ((BLK, 2 * HD), BF), ((BLK, 2 * HD), BF), ((BLK, 2 * HD), BF), ((BLK, 2 * HD), F32)
        scratch += [pltpu.VMEM(*w) for w in wide]
    else:
        wide = (((ROWS, HD), F32),) * 2
    outs = (shape((UNIT, HEADS * HD), BF),) * 4 + tuple(shape(*w) for w in wide)
    return pl.pallas_call(
        functools.partial(attention_kernel, last),
        out_shape=outs,
        in_specs=[pl.BlockSpec(memory_space=pltpu.SMEM)] + [hbm] * (8 + len(sums)),
        out_specs=(hbm,) * len(outs),
        scratch_shapes=scratch,
        compiler_params=pltpu.CompilerParams(vmem_limit_bytes=58 << 20),
        cost_estimate=pl.CostEstimate(
            flops=14_000_000_000, bytes_accessed=12 << 20, transcendentals=0
        ),
    )(info, *pieces, *blocks, *sums)


def shifted(block, by):
    peers = lax.axis_size("dp")
    pairs = [(i, i + by) for i in range(peers) if 0 <= i + by < peers]
    return lax.ppermute(block, "dp", pairs)


def exchanged(block):
    return lax.ppermute(block, "dp", [(i, i ^ 1) for i in range(lax.axis_size("dp"))])


def target(index, step):
    if abs(step) == 2 and index % 2:
        step = -step
    return (index + step) % UNITS


def round_by(block, step, back=False):
    if step == 0:
        return block
    pairs = [(i, target(i, step)) for i in range(UNITS)]
    return lax.ppermute(block, "sp", [(b, a) for a, b in pairs] if back else pairs)


def tables():
    sent = [{s: target(me, s) for s in STEPS[0] + STEPS[1]} for me in range(UNITS)]
    placed = []
    for me in range(UNITS):
        row = []
        for steps in STEPS:
            source = [next(i for i in range(UNITS) if target(i, s) == me) for s in steps]
            order = (0, 1, 2, 3) if me % 2 == 0 else (1, 2, 3, 0)
            for n in order:
                row += [n, source[n]]
        placed.append(row)
    return sent, placed


def all_to_all(array):
    return lax.all_to_all(array, "sp", split_axis=0, concat_axis=0, tiled=True)


def on_device(queries, grad_out, key_heads, value_heads, seq_start):
    even = lax.axis_index("dp") % 2 == 0
    window_first = lax.axis_index("dp") * BLK - PAST
    me = lax.axis_index("sp")
    by_head = lambda a: a.reshape(UNIT, HK, -1)
    sent, placed = tables()
    goes = {
        s: jnp.array([row[s] for row in sent], jnp.int32)[me] * HEADS * HD for s in sent[0]
    }
    part_of = lambda a, s: lax.dynamic_slice_in_dim(a, goes[s], HEADS * HD, 1)
    start = jnp.broadcast_to((seq_start[0] // UNIT).astype(BF), (HK, 16, 2 * HD))
    kv = jnp.concatenate([by_head(key_heads), by_head(value_heads)], axis=2).transpose(1, 0, 2)
    own = all_to_all(jnp.concatenate([kv, start], axis=1))
    units = {
        s: round_by(jnp.concatenate([part_of(queries, s), part_of(grad_out, s)], axis=1), s)
        for s in STEPS[0] + STEPS[1]
    }
    info = own[:, UNIT, 0].astype(F32).astype(jnp.int32) * UNIT - window_first
    info = jnp.concatenate([info, jnp.array(placed, jnp.int32)[me]])
    block = own[:, :UNIT].reshape(BLK, 2 * HD)
    h1 = shifted(block, 1)
    h3 = shifted(block, 3)
    near = [units[s] for s in STEPS[0]]
    h1, h3, *near = lax.optimization_barrier((h1, h3, *near))
    units.update(zip(STEPS[0], near))
    h2 = exchanged(jnp.where(even, h1, h3))
    grads, sums = {}, ()
    for last in (False, True):
        pieces = [units[s] for s in STEPS[last]]
        result = attend(last, info, pieces, (h3, h2, h1, block), sums)
        dq, sums = result[:4], result[4:]
        grads.update({s: round_by(piece, s, True) for s, piece in zip(STEPS[last], dq)})
    p3, p2, p1, mine = sums
    early = [grads[s] for s in STEPS[0]]
    p2, *early = lax.optimization_barrier((p2, *early))
    grads.update(zip(STEPS[0], early))
    swap = exchanged(p2).astype(F32)
    t1 = (p1.astype(F32) + jnp.where(even, swap, 0.0)).astype(BF)
    t3 = (p3.astype(F32) + jnp.where(even, 0.0, swap)).astype(BF)
    total = mine + shifted(t1, -1).astype(F32) + shifted(t3, -3).astype(F32)
    dkv = all_to_all(total.astype(BF).reshape(UNITS, UNIT, 2 * HD)).transpose(1, 0, 2)
    query_grad = jnp.zeros((UNIT, HQ * HD), BF)
    for s, piece in grads.items():
        query_grad = lax.dynamic_update_slice_in_dim(query_grad, piece, goes[s], 1)
    key_grad = dkv[:, :, :HD].reshape(UNIT, HK * HD)
    value_grad = dkv[:, :, HD:].reshape(UNIT, HK * HD)
    return (query_grad, key_grad, value_grad)


def solution(mesh):
    rows = P(("dp", "sp"), None)
    return jax.shard_map(
        on_device,
        mesh=mesh,
        in_specs=(rows, rows, rows, rows, P(("dp", "sp"))),
        out_specs=(rows, rows, rows),
        check_vma=False,
    )
```

profile of v0, /device:TPU:19, one launch (start us, length us, event | category | flops | bytes accessed | tf_op | source)
XLA Modules:
  0.0 172.8 jit_solution(561630460067865819)
XLA Ops:
  6.4 8.2 %all-to-all-start = ((bf16[8,144,256]{2,1,0:T(8,128)(2,1)}), bf16[8,144,256]{2,1,0:T(8,128)(2,1)S(1)}, u32[]{:S(2)}, u32[]{:S(2)}) async-start(bf16[8,144,256]{2,1,0:T(8,128)(2,1)} %concatenate.34), calls=%async_computation | async-start | bytes 1179648 | tf_op jit(solution)/shard_map/all_to_all | solution.py:240
  25.3 2.4 %collective-permute-start.6 = (bf16[128,1024]{1,0:T(8,128)(2,1)}, bf16[128,1024]{1,0:T(8,128)(2,1)}, u32[]{:S(2)}, u32[]{:S(2)}) collective-permute-start(bf16[128,1024]{1,0:T(8,128)(2,1)} %pad_maximum_fusion.5), channel_id=1, source_target_pairs={{0,2},{1,7},{2,4},{3,1},{4,6},{5,3},{6,0},{7,5},{8,10},{9,15},{10,... | collective-permute-start | bytes 786440 | tf_op jit(solution)/shard_map/ppermute | solution.py:222
  28.3 1.5 collective-permute-start.7
  29.8 4.1 %all-to-all-done = bf16[8,144,256]{2,1,0:T(8,128)(2,1)S(1)} async-done(((bf16[8,144,256]{2,1,0:T(8,128)(2,1)}), bf16[8,144,256]{2,1,0:T(8,128)(2,1)S(1)}, u32[]{:S(2)}, u32[]{:S(2)}) %all-to-all-start) | async-done | bytes 589856 | tf_op jit(solution)/shard_map/all_to_all | solution.py:240
  34.0 3.5 %collective-permute-start.4 = (bf16[1024,256]{1,0:T(8,128)(2,1)S(1)}, bf16[1024,256]{1,0:T(8,128)(2,1)S(1)}, u32[]{:S(2)}, u32[]{:S(2)}) collective-permute-start(bf16[1024,256]{1,0:T(8,128)(2,1)S(1)} %bitcast.37), channel_id=1, source_target_pairs={{0,8},{8,16},{16,24},{24,32},{32,40},{40,48},{48,56},{56,64},{64,7... | collective-permute-start | bytes 1572872 | tf_op jit(solution)/shard_map/ppermute | solution.py:205
  37.5 1.9 %collective-permute-start.5 = (bf16[1024,256]{1,0:T(8,128)(2,1)S(1)}, bf16[1024,256]{1,0:T(8,128)(2,1)S(1)}, u32[]{:S(2)}, u32[]{:S(2)}) collective-permute-start(bf16[1024,256]{1,0:T(8,128)(2,1)S(1)} %bitcast.38), channel_id=1, source_target_pairs={{0,24},{8,32},{16,40},{24,48},{32,56},{40,64},{48,72},{56,80},{64,... | collective-permute-start | bytes 1572872 | tf_op jit(solution)/shard_map/ppermute | solution.py:205
  39.5 1.7 pad_maximum_fusion.8
  43.8 2.0 %collective-permute-start.1 = (bf16[128,1024]{1,0:T(8,128)(2,1)}, bf16[128,1024]{1,0:T(8,128)(2,1)}, u32[]{:S(2)}, u32[]{:S(2)}) collective-permute-start(bf16[128,1024]{1,0:T(8,128)(2,1)} %pad_maximum_fusion.2), channel_id=1, source_target_pairs={{0,5},{1,6},{2,7},{3,0},{4,1},{5,2},{6,3},{7,4},{8,13},{9,14},{10,... | collective-permute-start | bytes 786440 | tf_op jit(solution)/shard_map/ppermute | solution.py:222
  45.8 2.3 %collective-permute-done.8.refs_3_ = bf16[128,1024]{1,0:T(8,128)(2,1)} collective-permute-done((bf16[128,1024]{1,0:T(8,128)(2,1)}, bf16[128,1024]{1,0:T(8,128)(2,1)}, u32[]{:S(2)}, u32[]{:S(2)}) %collective-permute-start.8) | collective-permute-done | bytes 262176 | tf_op jit(solution)/shard_map/ppermute | solution.py:222
  49.3 3.4 %collective-permute-done.4.refs_6_ = bf16[1024,256]{1,0:T(8,128)(2,1)S(1)} collective-permute-done((bf16[1024,256]{1,0:T(8,128)(2,1)S(1)}, bf16[1024,256]{1,0:T(8,128)(2,1)S(1)}, u32[]{:S(2)}, u32[]{:S(2)}) %collective-permute-start.4) | collective-permute-done | bytes 524320 | tf_op jit(solution)/shard_map/ppermute | solution.py:205
  52.7 3.5 %collective-permute-done.5.refs_4_ = bf16[1024,256]{1,0:T(8,128)(2,1)S(1)} collective-permute-done((bf16[1024,256]{1,0:T(8,128)(2,1)S(1)}, bf16[1024,256]{1,0:T(8,128)(2,1)S(1)}, u32[]{:S(2)}, u32[]{:S(2)}) %collective-permute-start.5) | collective-permute-done | bytes 524320 | tf_op jit(solution)/shard_map/ppermute | solution.py:205
  56.2 1.5 collective-permute-start.9
  59.5 20.0 %shard_map.157 = (bf16[128,512]{1,0:T(8,128)(2,1)}, bf16[128,512]{1,0:T(8,128)(2,1)}, bf16[128,512]{1,0:T(8,128)(2,1)}, bf16[128,512]{1,0:T(8,128)(2,1)}, f32[4608,128]{1,0:T(8,128)}, /*index=5*/f32[4608,128]{1,0:T(8,128)}) custom-call(s32[24]{0:T(128)} %pad_add_fusion.info_ref, bf16[128,1024]{1,0:T(8,128)(2,1)} %collective-permute-done.6.refs_0_, ...), custom_call_target="tpu_custom_call" | custom-call | flops 14000000000 | bytes 12582912 | tf_op jit(solution)/shard_map/pallas_call | solution.py:189
  79.6 6.8 %collective-permute-start.11 = (bf16[128,512]{1,0:T(8,128)(2,1)}, bf16[128,512]{1,0:T(8,128)(2,1)S(1)}, u32[]{:S(2)}, u32[]{:S(2)}) collective-permute-start(bf16[128,512]{1,0:T(8,128)(2,1)} %get-tuple-element.38), channel_id=1, source_target_pairs={{1,0},{2,1},{3,2},{4,3},{5,4},{6,5},{7,6},{0,7},{9,8},{10,9},{11,1... | collective-permute-start | bytes 393224 | tf_op jit(solution)/shard_map/ppermute | solution.py:222
  86.4 12.1 %shard_map.158 = (bf16[128,512]{1,0:T(8,128)(2,1)}, bf16[128,512]{1,0:T(8,128)(2,1)}, bf16[128,512]{1,0:T(8,128)(2,1)}, bf16[128,512]{1,0:T(8,128)(2,1)}, bf16[1...) custom-call(s32[24]{0:T(128)} %pad_add_fusion.info_ref, ...), custom_call_target="tpu_custom_call" | custom-call | flops 14000000000 | bytes 12582912 | tf_op jit(solution)/shard_map/pallas_call | solution.py:189
  98.6 10.7 %collective-permute-start.17 = (bf16[1024,256]{1,0:T(8,128)(2,1)}, bf16[1024,256]{1,0:T(8,128)(2,1)S(1)}, u32[]{:S(2)}, u32[]{:S(2)}) collective-permute-start(bf16[1024,256]{1,0:T(8,128)(2,1)} %get-tuple-element.51), channel_id=1, source_target_pairs={{0,8},{8,0},{16,24},{24,16},{32,40},{40,32},{48,56},{56,48},{64,72... | collective-permute-start | bytes 1572872 | tf_op jit(solution)/shard_map/ppermute | solution.py:209
  109.3 1.7 %collective-permute-done.17 = bf16[1024,256]{1,0:T(8,128)(2,1)S(1)} collective-permute-done((bf16[1024,256]{1,0:T(8,128)(2,1)}, bf16[1024,256]{1,0:T(8,128)(2,1)S(1)}, u32[]{:S(2)}, u32[]{:S(2)}) %collective-permute-start.17) | collective-permute-done | bytes 524320 | tf_op jit(solution)/shard_map/ppermute | solution.py:209
  112.5 2.3 %collective-permute-start.18 = (bf16[1024,256]{1,0:T(8,128)(2,1)S(1)}, bf16[1024,256]{1,0:T(8,128)(2,1)S(1)}, u32[]{:S(2)}, u32[]{:S(2)}) collective-permute-start(bf16[1024,256]{1,0:T(8,128)(2,1)S(1)} %get-tuple-element.71), channel_id=1, source_target_pairs={{8,0},{16,8},{24,16},{32,24},{40,32},{48,40},{56,48},{64,56},{72,6... | collective-permute-start | bytes 1572872 | tf_op jit(solution)/shard_map/ppermute | solution.py:205
  114.8 18.2 %collective-permute-start.19 = (bf16[1024,256]{1,0:T(8,128)(2,1)S(1)}, bf16[1024,256]{1,0:T(8,128)(2,1)S(1)}, u32[]{:S(2)}, u32[]{:S(2)}) collective-permute-start(bf16[1024,256]{1,0:T(8,128)(2,1)S(1)} %get-tuple-element.72), channel_id=1, source_target_pairs={{24,0},{32,8},{40,16},{48,24},{56,32},{64,40},{72,48},{80,56},{88,... | collective-permute-start | bytes 1572872 | tf_op jit(solution)/shard_map/ppermute | solution.py:205
  133.2 3.6 %collective-permute-start.15 = (bf16[128,512]{1,0:T(8,128)(2,1)S(1)}, bf16[128,512]{1,0:T(8,128)(2,1)S(1)}, u32[]{:S(2)}, u32[]{:S(2)}) collective-permute-start(bf16[128,512]{1,0:T(8,128)(2,1)S(1)} %copy-done.13), channel_id=1, source_target_pairs={{4,0},{5,1},{6,2},{7,3},{0,4},{1,5},{2,6},{3,7},{12,8},{13,9},{14,... | collective-permute-start | bytes 393224 | tf_op jit(solution)/shard_map/ppermute | solution.py:222
  136.8 2.4 %collective-permute-start.16 = (bf16[128,512]{1,0:T(8,128)(2,1)S(1)}, bf16[128,512]{1,0:T(8,128)(2,1)S(1)}, u32[]{:S(2)}, u32[]{:S(2)}) collective-permute-start(bf16[128,512]{1,0:T(8,128)(2,1)S(1)} %copy-done.12), channel_id=1, source_target_pairs={{3,0},{4,1},{5,2},{6,3},{7,4},{0,5},{1,6},{2,7},{11,8},{12,9},{13,... | collective-permute-start | bytes 393224 | tf_op jit(solution)/shard_map/ppermute | solution.py:222
  139.2 9.5 %collective-permute-done.19 = bf16[1024,256]{1,0:T(8,128)(2,1)S(1)} collective-permute-done((bf16[1024,256]{1,0:T(8,128)(2,1)S(1)}, bf16[1024,256]{1,0:T(8,128)(2,1)S(1)}, u32[]{:S(2)}, u32[]{:S(2)}) %collective-permute-start.19) | collective-permute-done | bytes 524320 | tf_op jit(solution)/shard_map/ppermute | solution.py:205
  149.6 3.5 %all-to-all-start.1 = ((bf16[8,128,256]{2,1,0:T(8,128)(2,1)}), bf16[8,128,256]{2,1,0:T(8,128)(2,1)S(1)}, u32[]{:S(2)}, u32[]{:S(2)}) async-start(bf16[8,128,256]{2,1,0:T(8,128)(2,1)} %bitcast.12), calls=%async_computation.1 | async-start | bytes 1048576 | tf_op jit(solution)/shard_map/all_to_all | solution.py:240
  153.5 17.6 %all-to-all-done.1 = bf16[8,128,256]{2,1,0:T(8,128)(2,1)S(1)} async-done(((bf16[8,128,256]{2,1,0:T(8,128)(2,1)}), bf16[8,128,256]{2,1,0:T(8,128)(2,1)S(1)}, u32[]{:S(2)}, u32[]{:S(2)}) %all-to-all-start.1) | async-done | bytes 524320 | tf_op jit(solution)/shard_map/all_to_all | solution.py:240
  (110 shorter events, 20.0 us)
Async XLA Ops:
  6.4 27.5 %all-to-all-start = ((bf16[8,144,256]{2,1,0:T(8,128)(2,1)}), bf16[8,144,256]{2,1,0:T(8,128)(2,1)S(1)}, u32[]{:S(2)}, u32[]{:S(2)}) async-start(bf16[8,144,256]{2,1,0:T(8,128)(2,1)} %concatenate.34), calls=%async_computation | async-start | bytes 1179648 | tf_op jit(solution)/shard_map/all_to_all | solution.py:240
  25.3 18.2 %collective-permute-start.6 = (bf16[128,1024]{1,0:T(8,128)(2,1)}, bf16[128,1024]{1,0:T(8,128)(2,1)}, u32[]{:S(2)}, u32[]{:S(2)}) collective-permute-start(bf16[128,1024]{1,0:T(8,128)(2,1)} %pad_maximum_fusion.5), channel_id=1, source_target_pairs={{0,2},{1,7},{2,4},{3,1},{4,6},{5,3},{6,0},{7,5},{8,10},{9,15},{10,... | collective-permute-start | bytes 786440 | tf_op jit(solution)/shard_map/ppermute | solution.py:222
  28.3 15.4 %collective-permute-start.7 = (bf16[128,1024]{1,0:T(8,128)(2,1)}, bf16[128,1024]{1,0:T(8,128)(2,1)}, u32[]{:S(2)}, u32[]{:S(2)}) collective-permute-start(bf16[128,1024]{1,0:T(8,128)(2,1)} %pad_maximum_fusion.6), channel_id=1, source_target_pairs={{0,1},{1,2},{2,3},{3,4},{4,5},{5,6},{6,7},{7,0},{8,9},{9,10},{10,1... | collective-permute-start | bytes 786440 | tf_op jit(solution)/shard_map/ppermute | solution.py:222
  34.0 18.7 %collective-permute-start.4 = (bf16[1024,256]{1,0:T(8,128)(2,1)S(1)}, bf16[1024,256]{1,0:T(8,128)(2,1)S(1)}, u32[]{:S(2)}, u32[]{:S(2)}) collective-permute-start(bf16[1024,256]{1,0:T(8,128)(2,1)S(1)} %bitcast.37), channel_id=1, source_target_pairs={{0,8},{8,16},{16,24},{24,32},{32,40},{40,48},{48,56},{56,64},{64,7... | collective-permute-start | bytes 1572872 | tf_op jit(solution)/shard_map/ppermute | solution.py:205
  37.5 18.6 %collective-permute-start.5 = (bf16[1024,256]{1,0:T(8,128)(2,1)S(1)}, bf16[1024,256]{1,0:T(8,128)(2,1)S(1)}, u32[]{:S(2)}, u32[]{:S(2)}) collective-permute-start(bf16[1024,256]{1,0:T(8,128)(2,1)S(1)} %bitcast.38), channel_id=1, source_target_pairs={{0,24},{8,32},{16,40},{24,48},{32,56},{40,64},{48,72},{56,80},{64,... | collective-permute-start | bytes 1572872 | tf_op jit(solution)/shard_map/ppermute | solution.py:205
  41.2 6.9 %collective-permute-start.8 = (bf16[128,1024]{1,0:T(8,128)(2,1)}, bf16[128,1024]{1,0:T(8,128)(2,1)}, u32[]{:S(2)}, u32[]{:S(2)}) collective-permute-start(bf16[128,1024]{1,0:T(8,128)(2,1)} %pad_maximum_fusion.8), channel_id=1, source_target_pairs={{0,7},{1,0},{2,1},{3,2},{4,3},{5,4},{6,5},{7,6},{8,15},{9,8},{10,9... | collective-permute-start | bytes 786440 | tf_op jit(solution)/shard_map/ppermute | solution.py:222
  43.5 36.1 %collective-permute-start = (bf16[128,1024]{1,0:T(8,128)(2,1)}, bf16[128,1024]{1,0:T(8,128)(2,1)}, u32[]{:S(2)}, u32[]{:S(2)}) collective-permute-start(bf16[128,1024]{1,0:T(8,128)(2,1)} %pad_maximum_fusion.1), channel_id=1, source_target_pairs={{0,6},{1,3},{2,0},{3,5},{4,2},{5,7},{6,4},{7,1},{8,14},{9,11},{10,... | collective-permute-start | bytes 786440 | tf_op jit(solution)/shard_map/ppermute | solution.py:222
  43.8 42.6 %collective-permute-start.1 = (bf16[128,1024]{1,0:T(8,128)(2,1)}, bf16[128,1024]{1,0:T(8,128)(2,1)}, u32[]{:S(2)}, u32[]{:S(2)}) collective-permute-start(bf16[128,1024]{1,0:T(8,128)(2,1)} %pad_maximum_fusion.2), channel_id=1, source_target_pairs={{0,5},{1,6},{2,7},{3,0},{4,1},{5,2},{6,3},{7,4},{8,13},{9,14},{10,... | collective-permute-start | bytes 786440 | tf_op jit(solution)/shard_map/ppermute | solution.py:222
  48.0 38.3 %collective-permute-start.2 = (bf16[128,1024]{1,0:T(8,128)(2,1)S(1)}, bf16[128,1024]{1,0:T(8,128)(2,1)}, u32[]{:S(2)}, u32[]{:S(2)}) collective-permute-start(bf16[128,1024]{1,0:T(8,128)(2,1)S(1)} %pad_maximum_fusion.3), channel_id=1, source_target_pairs={{0,4},{1,5},{2,6},{3,7},{4,0},{5,1},{6,2},{7,3},{8,12},{9,13},{10,... | collective-permute-start | bytes 786440 | tf_op jit(solution)/shard_map/ppermute | solution.py:222
  56.2 3.2 %collective-permute-start.9 = (bf16[1024,256]{1,0:T(8,128)(2,1)S(1)}, bf16[1024,256]{1,0:T(8,128)(2,1)}, u32[]{:S(2)}, u32[]{:S(2)}) collective-permute-start(bf16[1024,256]{1,0:T(8,128)(2,1)S(1)} %broadcast_select_fusion), channel_id=1, source_target_pairs={{0,8},{8,0},{16,24},{24,16},{32,40},{40,32},{48,56},{56,48},{64,72... | collective-permute-start | bytes 1572872 | tf_op jit(solution)/shard_map/ppermute | solution.py:209
  57.8 28.6 %collective-permute-start.3 = (bf16[128,1024]{1,0:T(8,128)(2,1)S(1)}, bf16[128,1024]{1,0:T(8,128)(2,1)}, u32[]{:S(2)}, u32[]{:S(2)}) collective-permute-start(bf16[128,1024]{1,0:T(8,128)(2,1)S(1)} %pad_maximum_fusion.4), channel_id=1, source_target_pairs={{0,3},{1,4},{2,5},{3,6},{4,7},{5,0},{6,1},{7,2},{8,11},{9,12},{10,... | collective-permute-start | bytes 786440 | tf_op jit(solution)/shard_map/ppermute | solution.py:222
  79.5 19.0 %collective-permute-start.10 = (bf16[128,512]{1,0:T(8,128)(2,1)}, bf16[128,512]{1,0:T(8,128)(2,1)S(1)}, u32[]{:S(2)}, u32[]{:S(2)}) collective-permute-start(bf16[128,512]{1,0:T(8,128)(2,1)} %get-tuple-element.37), channel_id=1, source_target_pairs={{2,0},{7,1},{4,2},{1,3},{6,4},{3,5},{0,6},{5,7},{10,8},{15,9},{12,... | collective-permute-start | bytes 393224 | tf_op jit(solution)/shard_map/ppermute | solution.py:222
  79.6 18.9 %collective-permute-start.11 = (bf16[128,512]{1,0:T(8,128)(2,1)}, bf16[128,512]{1,0:T(8,128)(2,1)S(1)}, u32[]{:S(2)}, u32[]{:S(2)}) collective-permute-start(bf16[128,512]{1,0:T(8,128)(2,1)} %get-tuple-element.38), channel_id=1, source_target_pairs={{1,0},{2,1},{3,2},{4,3},{5,4},{6,5},{7,6},{0,7},{9,8},{10,9},{11,1... | collective-permute-start | bytes 393224 | tf_op jit(solution)/shard_map/ppermute | solution.py:222
  86.4 12.2 %collective-permute-start.12 = (bf16[128,512]{1,0:T(8,128)(2,1)}, bf16[128,512]{1,0:T(8,128)(2,1)S(1)}, u32[]{:S(2)}, u32[]{:S(2)}) collective-permute-start(bf16[128,512]{1,0:T(8,128)(2,1)} %get-tuple-element.40), channel_id=1, source_target_pairs={{7,0},{0,1},{1,2},{2,3},{3,4},{4,5},{5,6},{6,7},{15,8},{8,9},{9,10... | collective-permute-start | bytes 393224 | tf_op jit(solution)/shard_map/ppermute | solution.py:222
  98.5 38.3 %copy-start.12 = (bf16[128,512]{1,0:T(8,128)(2,1)S(1)}, bf16[128,512]{1,0:T(8,128)(2,1)}, u32[]{:S(2)}) copy-start(bf16[128,512]{1,0:T(8,128)(2,1)} %get-tuple-element.48) | copy-start | bytes 393220
  98.5 50.2 %copy-start.2 = (f32[1024,256]{1,0:T(8,128)S(1)}, f32[1024,256]{1,0:T(8,128)}, u32[]{:S(2)}) copy-start(f32[1024,256]{1,0:T(8,128)} %get-tuple-element.49) | copy-start | bytes 3145732
  98.6 12.5 %collective-permute-start.17 = (bf16[1024,256]{1,0:T(8,128)(2,1)}, bf16[1024,256]{1,0:T(8,128)(2,1)S(1)}, u32[]{:S(2)}, u32[]{:S(2)}) collective-permute-start(bf16[1024,256]{1,0:T(8,128)(2,1)} %get-tuple-element.51), channel_id=1, source_target_pairs={{0,8},{8,0},{16,24},{24,16},{32,40},{40,32},{48,56},{56,48},{64,72... | collective-permute-start | bytes 1572872 | tf_op jit(solution)/shard_map/ppermute | solution.py:209
  112.5 24.3 %collective-permute-start.18 = (bf16[1024,256]{1,0:T(8,128)(2,1)S(1)}, bf16[1024,256]{1,0:T(8,128)(2,1)S(1)}, u32[]{:S(2)}, u32[]{:S(2)}) collective-permute-start(bf16[1024,256]{1,0:T(8,128)(2,1)S(1)} %get-tuple-element.71), channel_id=1, source_target_pairs={{8,0},{16,8},{24,16},{32,24},{40,32},{48,40},{56,48},{64,56},{72,6... | collective-permute-start | bytes 1572872 | tf_op jit(solution)/shard_map/ppermute | solution.py:205
  114.8 33.9 %collective-permute-start.19 = (bf16[1024,256]{1,0:T(8,128)(2,1)S(1)}, bf16[1024,256]{1,0:T(8,128)(2,1)S(1)}, u32[]{:S(2)}, u32[]{:S(2)}) collective-permute-start(bf16[1024,256]{1,0:T(8,128)(2,1)S(1)} %get-tuple-element.72), channel_id=1, source_target_pairs={{24,0},{32,8},{40,16},{48,24},{56,32},{64,40},{72,48},{80,56},{88,... | collective-permute-start | bytes 1572872 | tf_op jit(solution)/shard_map/ppermute | solution.py:205
  133.0 20.4 %collective-permute-start.13 = (bf16[128,512]{1,0:T(8,128)(2,1)S(1)}, bf16[128,512]{1,0:T(8,128)(2,1)S(1)}, u32[]{:S(2)}, u32[]{:S(2)}) collective-permute-start(bf16[128,512]{1,0:T(8,128)(2,1)S(1)} %copy-done.15), channel_id=1, source_target_pairs={{6,0},{3,1},{0,2},{5,3},{2,4},{7,5},{4,6},{1,7},{14,8},{11,9},{8,1... | collective-permute-start | bytes 393224 | tf_op jit(solution)/shard_map/ppermute | solution.py:222
  133.1 20.3 %collective-permute-start.14 = (bf16[128,512]{1,0:T(8,128)(2,1)S(1)}, bf16[128,512]{1,0:T(8,128)(2,1)S(1)}, u32[]{:S(2)}, u32[]{:S(2)}) collective-permute-start(bf16[128,512]{1,0:T(8,128)(2,1)S(1)} %copy-done.14), channel_id=1, source_target_pairs={{5,0},{6,1},{7,2},{0,3},{1,4},{2,5},{3,6},{4,7},{13,8},{14,9},{15,... | collective-permute-start | bytes 393224 | tf_op jit(solution)/shard_map/ppermute | solution.py:222
  133.2 20.3 %collective-permute-start.15 = (bf16[128,512]{1,0:T(8,128)(2,1)S(1)}, bf16[128,512]{1,0:T(8,128)(2,1)S(1)}, u32[]{:S(2)}, u32[]{:S(2)}) collective-permute-start(bf16[128,512]{1,0:T(8,128)(2,1)S(1)} %copy-done.13), channel_id=1, source_target_pairs={{4,0},{5,1},{6,2},{7,3},{0,4},{1,5},{2,6},{3,7},{12,8},{13,9},{14,... | collective-permute-start | bytes 393224 | tf_op jit(solution)/shard_map/ppermute | solution.py:222
  136.8 16.7 %collective-permute-start.16 = (bf16[128,512]{1,0:T(8,128)(2,1)S(1)}, bf16[128,512]{1,0:T(8,128)(2,1)S(1)}, u32[]{:S(2)}, u32[]{:S(2)}) collective-permute-start(bf16[128,512]{1,0:T(8,128)(2,1)S(1)} %copy-done.12), channel_id=1, source_target_pairs={{3,0},{4,1},{5,2},{6,3},{7,4},{0,5},{1,6},{2,7},{11,8},{12,9},{13,... | collective-permute-start | bytes 393224 | tf_op jit(solution)/shard_map/ppermute | solution.py:222
  149.6 21.4 %all-to-all-start.1 = ((bf16[8,128,256]{2,1,0:T(8,128)(2,1)}), bf16[8,128,256]{2,1,0:T(8,128)(2,1)S(1)}, u32[]{:S(2)}, u32[]{:S(2)}) async-start(bf16[8,128,256]{2,1,0:T(8,128)(2,1)} %bitcast.12), calls=%async_computation.1 | async-start | bytes 1048576 | tf_op jit(solution)/shard_map/all_to_all | solution.py:240
  (21 other events, 362.3 us)
where the time goes:
time: 173 us
  starting transfers between devices  70.5 us (41%)
  waiting for transfers between devices  42.1 us (24%)
  Pallas kernels  32.1 us (19%)
  local copies, waits for them, and re-layouts  11 us (6%)
  other arithmetic  8.58 us (5%)
  between operations  8.46 us (5%)
    pallas_call x2, Pallas kernels, attend(): pl.pallas_call(functools.partial(attention_kernel, last), out_shape=outs,...  32.1 us
    ppermute x4, starting transfers between devices, shifted(): return lax.ppermute(block, 'dp', pairs)  25.9 us
    all_to_all x2, waiting for transfers between devices, all_to_all(): return lax.all_to_all(array, 'sp', split_axis=0, concat_axis=0, tiled=True)  21.7 us
    ppermute x14, starting transfers between devices, round_by(): lax.ppermute(block, 'sp', [(b, a) for a, b in pairs] if back else pairs)  20.7 us
    ppermute x4, waiting for transfers between devices, shifted(): return lax.ppermute(block, 'dp', pairs)  16.4 us
    ppermute x2, starting transfers between devices, exchanged(): lax.ppermute(block, 'dp', [(i, i ^ 1) for i in range(lax.axis_size('dp'))])  12.2 us
    all_to_all x2, starting transfers between devices, all_to_all(): return lax.all_to_all(array, 'sp', split_axis=0, concat_axis=0, tiled=True)  11.7 us
    concatenate x8, other arithmetic, on_device(): jnp.concatenate([part_of(queries, s), part_of(grad_out, s)], axis=1)  5.42 us
  transfers between devices with their start and end apart: 22, of which 7 were waited for; matrix products, arithmetic and copies ran while one was open for 8% of the time, Pallas kernels for 19%

commit v1 on v0

--- a/solution.py
+++ b/solution.py
@@ -48,17 +48,18 @@
         rows = pl.ds(at * BLK, BLK)
         loads.append((block.at[:, pl.ds(0, HD)], kbuf.at[rows, :]))
         loads.append((block.at[:, pl.ds(HD, HD)], vbuf.at[rows, :]))
+    late = len(loads)
     if last:
-        loads += [(sums[0], dkacc), (sums[1], dvacc)]
+        *wide, sum_k, sum_v = wide
+        loads += [(sums[0], sum_k), (sums[1], sum_v)]
     loads = [pltpu.make_async_copy(a, b, in_sem.at[n]) for n, (a, b) in enumerate(loads)]
     for copy in loads:
         copy.start()
     kbuf[SPAN * BLK :, :] = jnp.zeros((CHUNK, HD), BF)
     vbuf[SPAN * BLK :, :] = jnp.zeros((CHUNK, HD), BF)
-    if not last:
-        dkacc[...] = jnp.zeros_like(dkacc)
-        dvacc[...] = jnp.zeros_like(dvacc)
-    for copy in loads:
+    dkacc[...] = jnp.zeros_like(dkacc)
+    dvacc[...] = jnp.zeros_like(dvacc)
+    for copy in loads[:late]:
         copy.wait()
     lane = lax.broadcasted_iota(jnp.int32, (1, LANES), 1) & (TILE - 1)
 
@@ -151,10 +152,12 @@
     for m, out in enumerate(dq_refs):
         store(dqbuf.at[m], out)
     if last:
+        for copy in loads[late:]:
+            copy.wait()
         for at, (held, out) in enumerate(zip(wide, outs)):
-            low = at * BLK
-            held[:, :HD] = (dkacc[low : low + BLK, :] * SCALE).astype(out.dtype)
-            held[:, HD:] = dvacc[low : low + BLK, :].astype(out.dtype)
+            here = slice(at * BLK, (at + 1) * BLK)
+            held[:, :HD] = ((dkacc[here, :] + sum_k[here, :]) * SCALE).astype(out.dtype)
+            held[:, HD:] = (dvacc[here, :] + sum_v[here, :]).astype(out.dtype)
             store(held, out)
     else:
         store(dkacc, outs[0])
@@ -182,7 +185,7 @@
     ]
     if last:
         wide = ((BLK, 2 * HD), BF), ((BLK, 2 * HD), BF), ((BLK, 2 * HD), BF), ((BLK, 2 * HD), F32)
-        scratch += [pltpu.VMEM(*w) for w in wide]
+        scratch += [pltpu.VMEM(*w) for w in wide] + [pltpu.VMEM((ROWS, HD), F32)] * 2
     else:
         wide = (((ROWS, HD), F32),) * 2
     outs = (shape((UNIT, HEADS * HD), BF),) * 4 + tuple(shape(*w) for w in wide)
@@ -192,7 +195,7 @@
         in_specs=[pl.BlockSpec(memory_space=pltpu.SMEM)] + [hbm] * (8 + len(sums)),
         out_specs=(hbm,) * len(outs),
         scratch_shapes=scratch,
-        compiler_params=pltpu.CompilerParams(vmem_limit_bytes=58 << 20),
+        compiler_params=pltpu.CompilerParams(vmem_limit_bytes=60 << 20),
         cost_estimate=pl.CostEstimate(
             flops=14_000_000_000, bytes_accessed=12 << 20, transcendentals=0
         ),
@@ -271,14 +274,14 @@
         pieces = [units[s] for s in STEPS[last]]
         result = attend(last, info, pieces, (h3, h2, h1, block), sums)
         dq, sums = result[:4], result[4:]
-        grads.update({s: round_by(piece, s, True) for s, piece in zip(STEPS[last], dq)})
+        grads.update(zip(STEPS[last], dq))
     p3, p2, p1, mine = sums
-    early = [grads[s] for s in STEPS[0]]
-    p2, *early = lax.optimization_barrier((p2, *early))
-    grads.update(zip(STEPS[0], early))
     swap = exchanged(p2).astype(F32)
     t1 = (p1.astype(F32) + jnp.where(even, swap, 0.0)).astype(BF)
     t3 = (p3.astype(F32) + jnp.where(even, 0.0, swap)).astype(BF)
+    order = sorted(grads, key=abs, reverse=True)
+    t1, t3, *pieces = lax.optimization_barrier((t1, t3, *[grads[s] for s in order]))
+    grads = {s: round_by(piece, s, True) for s, piece in zip(order, pieces)}
     total = mine + shifted(t1, -1).astype(F32) + shifted(t3, -3).astype(F32)
     dkv = all_to_all(total.astype(BF).reshape(UNITS, UNIT, 2 * HD)).transpose(1, 0, 2)
     query_grad = jnp.zeros((UNIT, HQ * HD), BF)

time: 173 us -> 167 us (0.965)
  starting transfers between devices: 70.5 us -> 57.3 us
  waiting for transfers between devices: 42.1 us -> 46.7 us
    all_to_all x2, waiting for transfers between devices: 21.7 us -> 6.18 us  [all_to_all(): return lax.all_to_all(array, 'sp', split_axis=0, concat_axis=0, tiled=True)]
    ppermute x14, waiting for transfers between devices: 2.3 us -> 15.5 us  [round_by(): lax.ppermute(block, 'sp', [(b, a) for a, b in pairs] if back else pairs)]
    ppermute x4, starting transfers between devices: 25.9 us -> 15.1 us  [shifted(): return lax.ppermute(block, 'dp', pairs)]
    ppermute x2, starting transfers between devices: 12.2 us -> 1.62 us  [exchanged(): lax.ppermute(block, 'dp', [(i, i ^ 1) for i in range(lax.axis_size('dp'))])]
    ppermute x4, waiting for transfers between devices: 16.4 us -> 22.9 us  [shifted(): return lax.ppermute(block, 'dp', pairs)]
    ppermute x14, starting transfers between devices: 20.7 us -> 25.8 us  [round_by(): lax.ppermute(block, 'sp', [(b, a) for a, b in pairs] if back else pairs)]
    all_to_all x2, starting transfers between devices: 11.7 us -> 14.8 us  [all_to_all(): return lax.all_to_all(array, 'sp', split_axis=0, concat_axis=0, tiled=True)]
  transfers between devices with their start and end apart: 22 -> 22, of which waited for: 7 -> 11; matrix products, arithmetic and copies ran while one was open for 8% -> 8% of each run, Pallas kernels for 19% -> 10%
where the time goes in v1:
time: 167 us; the launch traced here: 166 us
  starting transfers between devices  57.3 us (34%)
  waiting for transfers between devices  46.7 us (28%)
  Pallas kernels  33.6 us (20%)
  local copies, waits for them, and re-layouts  11 us (7%)
  other arithmetic  8.57 us (5%)
  between operations  8.44 us (5%)
    pallas_call x2, Pallas kernels, attend(): pl.pallas_call(functools.partial(attention_kernel, last), out_shape=outs,...  33.6 us
    ppermute x14, starting transfers between devices, round_by(): lax.ppermute(block, 'sp', [(b, a) for a, b in pairs] if back else pairs)  25.8 us
    ppermute x4, waiting for transfers between devices, shifted(): return lax.ppermute(block, 'dp', pairs)  22.9 us
    ppermute x14, waiting for transfers between devices, round_by(): lax.ppermute(block, 'sp', [(b, a) for a, b in pairs] if back else pairs)  15.5 us
    ppermute x4, starting transfers between devices, shifted(): return lax.ppermute(block, 'dp', pairs)  15.1 us
    all_to_all x2, starting transfers between devices, all_to_all(): return lax.all_to_all(array, 'sp', split_axis=0, concat_axis=0, tiled=True)  14.8 us
    all_to_all x2, waiting for transfers between devices, all_to_all(): return lax.all_to_all(array, 'sp', split_axis=0, concat_axis=0, tiled=True)  6.18 us
    concatenate x8, other arithmetic, on_device(): jnp.concatenate([part_of(queries, s), part_of(grad_out, s)], axis=1)  5.4 us
  transfers between devices with their start and end apart: 22, of which 11 were waited for; matrix products, arithmetic and copies ran while one was open for 8% of the time, Pallas kernels for 10%

profile of v1, /device:TPU:19, one launch (start us, length us, event | category | flops | bytes accessed | tf_op | source)
XLA Modules:
  0.0 165.6 jit_solution(5007346342764441213)
XLA Ops:
  6.4 8.2 %all-to-all-start = ((bf16[8,144,256]{2,1,0:T(8,128)(2,1)}), bf16[8,144,256]{2,1,0:T(8,128)(2,1)S(1)}, u32[]{:S(2)}, u32[]{:S(2)}) async-start(bf16[8,144,256]{2,1,0:T(8,128)(2,1)} %concatenate.34), calls=%async_computation | async-start | bytes 1179648 | tf_op jit(solution)/shard_map/all_to_all | solution.py:243
  25.2 2.4 %collective-permute-start.6 = (bf16[128,1024]{1,0:T(8,128)(2,1)}, bf16[128,1024]{1,0:T(8,128)(2,1)}, u32[]{:S(2)}, u32[]{:S(2)}) collective-permute-start(bf16[128,1024]{1,0:T(8,128)(2,1)} %pad_maximum_fusion.5), channel_id=1, source_target_pairs={{0,2},{1,7},{2,4},{3,1},{4,6},{5,3},{6,0},{7,5},{8,10},{9,15},{10,... | collective-permute-start | bytes 786440 | tf_op jit(solution)/shard_map/ppermute | solution.py:225
  29.8 4.1 %all-to-all-done = bf16[8,144,256]{2,1,0:T(8,128)(2,1)S(1)} async-done(((bf16[8,144,256]{2,1,0:T(8,128)(2,1)}), bf16[8,144,256]{2,1,0:T(8,128)(2,1)S(1)}, u32[]{:S(2)}, u32[]{:S(2)}) %all-to-all-start) | async-done | bytes 589856 | tf_op jit(solution)/shard_map/all_to_all | solution.py:243
  34.0 3.5 %collective-permute-start.4 = (bf16[1024,256]{1,0:T(8,128)(2,1)S(1)}, bf16[1024,256]{1,0:T(8,128)(2,1)S(1)}, u32[]{:S(2)}, u32[]{:S(2)}) collective-permute-start(bf16[1024,256]{1,0:T(8,128)(2,1)S(1)} %bitcast.37), channel_id=1, source_target_pairs={{0,8},{8,16},{16,24},{24,32},{32,40},{40,48},{48,56},{56,64},{64,7... | collective-permute-start | bytes 1572872 | tf_op jit(solution)/shard_map/ppermute | solution.py:208
  37.5 1.9 %collective-permute-start.5 = (bf16[1024,256]{1,0:T(8,128)(2,1)S(1)}, bf16[1024,256]{1,0:T(8,128)(2,1)S(1)}, u32[]{:S(2)}, u32[]{:S(2)}) collective-permute-start(bf16[1024,256]{1,0:T(8,128)(2,1)S(1)} %bitcast.38), channel_id=1, source_target_pairs={{0,24},{8,32},{16,40},{24,48},{32,56},{40,64},{48,72},{56,80},{64,... | collective-permute-start | bytes 1572872 | tf_op jit(solution)/shard_map/ppermute | solution.py:208
  43.7 2.0 %collective-permute-start.1 = (bf16[128,1024]{1,0:T(8,128)(2,1)}, bf16[128,1024]{1,0:T(8,128)(2,1)}, u32[]{:S(2)}, u32[]{:S(2)}) collective-permute-start(bf16[128,1024]{1,0:T(8,128)(2,1)} %pad_maximum_fusion.2), channel_id=1, source_target_pairs={{0,5},{1,6},{2,7},{3,0},{4,1},{5,2},{6,3},{7,4},{8,13},{9,14},{10,... | collective-permute-start | bytes 786440 | tf_op jit(solution)/shard_map/ppermute | solution.py:225
  45.8 2.3 %collective-permute-done.8.refs_3_ = bf16[128,1024]{1,0:T(8,128)(2,1)} collective-permute-done((bf16[128,1024]{1,0:T(8,128)(2,1)}, bf16[128,1024]{1,0:T(8,128)(2,1)}, u32[]{:S(2)}, u32[]{:S(2)}) %collective-permute-start.8) | collective-permute-done | bytes 262176 | tf_op jit(solution)/shard_map/ppermute | solution.py:225
  49.3 3.4 %collective-permute-done.4.refs_6_ = bf16[1024,256]{1,0:T(8,128)(2,1)S(1)} collective-permute-done((bf16[1024,256]{1,0:T(8,128)(2,1)S(1)}, bf16[1024,256]{1,0:T(8,128)(2,1)S(1)}, u32[]{:S(2)}, u32[]{:S(2)}) %collective-permute-start.4) | collective-permute-done | bytes 524320 | tf_op jit(solution)/shard_map/ppermute | solution.py:208
  52.7 3.5 %collective-permute-done.5.refs_4_ = bf16[1024,256]{1,0:T(8,128)(2,1)S(1)} collective-permute-done((bf16[1024,256]{1,0:T(8,128)(2,1)S(1)}, bf16[1024,256]{1,0:T(8,128)(2,1)S(1)}, u32[]{:S(2)}, u32[]{:S(2)}) %collective-permute-start.5) | collective-permute-done | bytes 524320 | tf_op jit(solution)/shard_map/ppermute | solution.py:208
  59.5 17.2 %shard_map.157 = (bf16[128,512]{1,0:T(8,128)(2,1)}, bf16[128,512]{1,0:T(8,128)(2,1)}, bf16[128,512]{1,0:T(8,128)(2,1)}, bf16[128,512]{1,0:T(8,128)(2,1)}, f32[4608,128]{1,0:T(8,128)}, /*index=5*/f32[4608,128]{1,0:T(8,128)}) custom-call(s32[24]{0:T(128)} %pad_add_fusion.info_ref, bf16[128,1024]{1,0:T(8,128)(2,1)} %collective-permute-done.6.refs_0_, ...), custom_call_target="tpu_custom_call" | custom-call | flops 14000000000 | bytes 12582912 | tf_op jit(solution)/shard_map/pallas_call | solution.py:192
  76.7 6.2 %collective-permute-done.3.refs_3_ = bf16[128,1024]{1,0:T(8,128)(2,1)} collective-permute-done((bf16[128,1024]{1,0:T(8,128)(2,1)S(1)}, bf16[128,1024]{1,0:T(8,128)(2,1)}, u32[]{:S(2)}, u32[]{:S(2)}) %collective-permute-start.3) | collective-permute-done | bytes 262176 | tf_op jit(solution)/shard_map/ppermute | solution.py:225
  82.9 16.5 %shard_map.158 = (bf16[128,512]{1,0:T(8,128)(2,1)}, bf16[128,512]{1,0:T(8,128)(2,1)}, bf16[128,512]{1,0:T(8,128)(2,1)}, bf16[128,512]{1,0:T(8,128)(2,1)}, bf16[1...) custom-call(s32[24]{0:T(128)} %pad_add_fusion.info_ref, ...), custom_call_target="tpu_custom_call" | custom-call | flops 14000000000 | bytes 12582912 | tf_op jit(solution)/shard_map/pallas_call | solution.py:192
  99.6 2.1 %collective-permute-done.10 = bf16[1024,256]{1,0:T(8,128)(2,1)S(1)} collective-permute-done((bf16[1024,256]{1,0:T(8,128)(2,1)}, bf16[1024,256]{1,0:T(8,128)(2,1)S(1)}, u32[]{:S(2)}, u32[]{:S(2)}) %collective-permute-start.10) | collective-permute-done | bytes 524320 | tf_op jit(solution)/shard_map/ppermute | solution.py:212
  103.2 2.2 %collective-permute-start.18 = (bf16[1024,256]{1,0:T(8,128)(2,1)S(1)}, bf16[1024,256]{1,0:T(8,128)(2,1)S(1)}, u32[]{:S(2)}, u32[]{:S(2)}) collective-permute-start(bf16[1024,256]{1,0:T(8,128)(2,1)S(1)} %get-tuple-element.61), channel_id=1, source_target_pairs={{8,0},{16,8},{24,16},{32,24},{40,32},{48,40},{56,48},{64,56},{72,6... | collective-permute-start | bytes 1572872 | tf_op jit(solution)/shard_map/ppermute | solution.py:208
  105.3 7.5 %collective-permute-start.19 = (bf16[1024,256]{1,0:T(8,128)(2,1)S(1)}, bf16[1024,256]{1,0:T(8,128)(2,1)S(1)}, u32[]{:S(2)}, u32[]{:S(2)}) collective-permute-start(bf16[1024,256]{1,0:T(8,128)(2,1)S(1)} %get-tuple-element.62), channel_id=1, source_target_pairs={{24,0},{32,8},{40,16},{48,24},{56,32},{64,40},{72,48},{80,56},{88,... | collective-permute-start | bytes 1572872 | tf_op jit(solution)/shard_map/ppermute | solution.py:208
  112.8 5.1 %collective-permute-start.11 = (bf16[128,512]{1,0:T(8,128)(2,1)S(1)}, bf16[128,512]{1,0:T(8,128)(2,1)S(1)}, u32[]{:S(2)}, u32[]{:S(2)}) collective-permute-start(bf16[128,512]{1,0:T(8,128)(2,1)S(1)} %copy-done.18), channel_id=1, source_target_pairs={{4,0},{5,1},{6,2},{7,3},{0,4},{1,5},{2,6},{3,7},{12,8},{13,9},{14,... | collective-permute-start | bytes 393224 | tf_op jit(solution)/shard_map/ppermute | solution.py:225
  118.9 3.5 %collective-permute-start.13 = (bf16[128,512]{1,0:T(8,128)(2,1)S(1)}, bf16[128,512]{1,0:T(8,128)(2,1)S(1)}, u32[]{:S(2)}, u32[]{:S(2)}) collective-permute-start(bf16[128,512]{1,0:T(8,128)(2,1)S(1)} %copy-done.16), channel_id=1, source_target_pairs={{3,0},{4,1},{5,2},{6,3},{7,4},{0,5},{1,6},{2,7},{11,8},{12,9},{13,... | collective-permute-start | bytes 393224 | tf_op jit(solution)/shard_map/ppermute | solution.py:225
  122.4 4.9 %collective-permute-done.18 = bf16[1024,256]{1,0:T(8,128)(2,1)S(1)} collective-permute-done((bf16[1024,256]{1,0:T(8,128)(2,1)S(1)}, bf16[1024,256]{1,0:T(8,128)(2,1)S(1)}, u32[]{:S(2)}, u32[]{:S(2)}) %collective-permute-start.18) | collective-permute-done | bytes 524320 | tf_op jit(solution)/shard_map/ppermute | solution.py:208
  127.3 4.3 %collective-permute-start.14 = (bf16[128,512]{1,0:T(8,128)(2,1)S(1)}, bf16[128,512]{1,0:T(8,128)(2,1)S(1)}, u32[]{:S(2)}, u32[]{:S(2)}) collective-permute-start(bf16[128,512]{1,0:T(8,128)(2,1)S(1)} %copy-done.14), channel_id=1, source_target_pairs={{2,0},{7,1},{4,2},{1,3},{6,4},{3,5},{0,6},{5,7},{10,8},{15,9},{12,... | collective-permute-start | bytes 393224 | tf_op jit(solution)/shard_map/ppermute | solution.py:225
  131.6 11.1 %collective-permute-done.19 = bf16[1024,256]{1,0:T(8,128)(2,1)S(1)} collective-permute-done((bf16[1024,256]{1,0:T(8,128)(2,1)S(1)}, bf16[1024,256]{1,0:T(8,128)(2,1)S(1)}, u32[]{:S(2)}, u32[]{:S(2)}) %collective-permute-start.19) | collective-permute-done | bytes 524320 | tf_op jit(solution)/shard_map/ppermute | solution.py:208
  145.1 6.6 %all-to-all-start.1 = ((bf16[8,128,256]{2,1,0:T(8,128)(2,1)}), bf16[8,128,256]{2,1,0:T(8,128)(2,1)S(1)}, u32[]{:S(2)}, u32[]{:S(2)}) async-start(bf16[8,128,256]{2,1,0:T(8,128)(2,1)} %bitcast.12), calls=%async_computation.1 | async-start | bytes 1048576 | tf_op jit(solution)/shard_map/all_to_all | solution.py:243
  151.7 2.7 %collective-permute-start.16 = (bf16[128,512]{1,0:T(8,128)(2,1)S(1)}, bf16[128,512]{1,0:T(8,128)(2,1)S(1)}, u32[]{:S(2)}, u32[]{:S(2)}) collective-permute-start(bf16[128,512]{1,0:T(8,128)(2,1)S(1)} %copy-done.13), channel_id=1, source_target_pairs={{1,0},{2,1},{3,2},{4,3},{5,4},{6,5},{7,6},{0,7},{9,8},{10,9},{11,1... | collective-permute-start | bytes 393224 | tf_op jit(solution)/shard_map/ppermute | solution.py:225
  154.8 6.5 %collective-permute-done.16 = bf16[128,512]{1,0:T(8,128)(2,1)S(1)} collective-permute-done((bf16[128,512]{1,0:T(8,128)(2,1)S(1)}, bf16[128,512]{1,0:T(8,128)(2,1)S(1)}, u32[]{:S(2)}, u32[]{:S(2)}) %collective-permute-start.16) | collective-permute-done | bytes 131104 | tf_op jit(solution)/shard_map/ppermute | solution.py:225
  161.9 2.0 %all-to-all-done.1 = bf16[8,128,256]{2,1,0:T(8,128)(2,1)S(1)} async-done(((bf16[8,128,256]{2,1,0:T(8,128)(2,1)}), bf16[8,128,256]{2,1,0:T(8,128)(2,1)S(1)}, u32[]{:S(2)}, u32[]{:S(2)}) %all-to-all-start.1) | async-done | bytes 524320 | tf_op jit(solution)/shard_map/all_to_all | solution.py:243
  (116 shorter events, 27.5 us)
Async XLA Ops:
  6.4 27.5 %all-to-all-start = ((bf16[8,144,256]{2,1,0:T(8,128)(2,1)}), bf16[8,144,256]{2,1,0:T(8,128)(2,1)S(1)}, u32[]{:S(2)}, u32[]{:S(2)}) async-start(bf16[8,144,256]{2,1,0:T(8,128)(2,1)} %concatenate.34), calls=%async_computation | async-start | bytes 1179648 | tf_op jit(solution)/shard_map/all_to_all | solution.py:243
  25.2 18.2 %collective-permute-start.6 = (bf16[128,1024]{1,0:T(8,128)(2,1)}, bf16[128,1024]{1,0:T(8,128)(2,1)}, u32[]{:S(2)}, u32[]{:S(2)}) collective-permute-start(bf16[128,1024]{1,0:T(8,128)(2,1)} %pad_maximum_fusion.5), channel_id=1, source_target_pairs={{0,2},{1,7},{2,4},{3,1},{4,6},{5,3},{6,0},{7,5},{8,10},{9,15},{10,... | collective-permute-start | bytes 786440 | tf_op jit(solution)/shard_map/ppermute | solution.py:225
  28.3 15.4 %collective-permute-start.7 = (bf16[128,1024]{1,0:T(8,128)(2,1)}, bf16[128,1024]{1,0:T(8,128)(2,1)}, u32[]{:S(2)}, u32[]{:S(2)}) collective-permute-start(bf16[128,1024]{1,0:T(8,128)(2,1)} %pad_maximum_fusion.6), channel_id=1, source_target_pairs={{0,1},{1,2},{2,3},{3,4},{4,5},{5,6},{6,7},{7,0},{8,9},{9,10},{10,1... | collective-permute-start | bytes 786440 | tf_op jit(solution)/shard_map/ppermute | solution.py:225
  34.0 18.7 %collective-permute-start.4 = (bf16[1024,256]{1,0:T(8,128)(2,1)S(1)}, bf16[1024,256]{1,0:T(8,128)(2,1)S(1)}, u32[]{:S(2)}, u32[]{:S(2)}) collective-permute-start(bf16[1024,256]{1,0:T(8,128)(2,1)S(1)} %bitcast.37), channel_id=1, source_target_pairs={{0,8},{8,16},{16,24},{24,32},{32,40},{40,48},{48,56},{56,64},{64,7... | collective-permute-start | bytes 1572872 | tf_op jit(solution)/shard_map/ppermute | solution.py:208
  37.5 18.6 %collective-permute-start.5 = (bf16[1024,256]{1,0:T(8,128)(2,1)S(1)}, bf16[1024,256]{1,0:T(8,128)(2,1)S(1)}, u32[]{:S(2)}, u32[]{:S(2)}) collective-permute-start(bf16[1024,256]{1,0:T(8,128)(2,1)S(1)} %bitcast.38), channel_id=1, source_target_pairs={{0,24},{8,32},{16,40},{24,48},{32,56},{40,64},{48,72},{56,80},{64,... | collective-permute-start | bytes 1572872 | tf_op jit(solution)/shard_map/ppermute | solution.py:208
  41.2 6.9 %collective-permute-start.8 = (bf16[128,1024]{1,0:T(8,128)(2,1)}, bf16[128,1024]{1,0:T(8,128)(2,1)}, u32[]{:S(2)}, u32[]{:S(2)}) collective-permute-start(bf16[128,1024]{1,0:T(8,128)(2,1)} %pad_maximum_fusion.8), channel_id=1, source_target_pairs={{0,7},{1,0},{2,1},{3,2},{4,3},{5,4},{6,5},{7,6},{8,15},{9,8},{10,9... | collective-permute-start | bytes 786440 | tf_op jit(solution)/shard_map/ppermute | solution.py:225
  43.4 33.3 %collective-permute-start = (bf16[128,1024]{1,0:T(8,128)(2,1)}, bf16[128,1024]{1,0:T(8,128)(2,1)}, u32[]{:S(2)}, u32[]{:S(2)}) collective-permute-start(bf16[128,1024]{1,0:T(8,128)(2,1)} %pad_maximum_fusion.1), channel_id=1, source_target_pairs={{0,6},{1,3},{2,0},{3,5},{4,2},{5,7},{6,4},{7,1},{8,14},{9,11},{10,... | collective-permute-start | bytes 786440 | tf_op jit(solution)/shard_map/ppermute | solution.py:225
  43.7 33.0 %collective-permute-start.1 = (bf16[128,1024]{1,0:T(8,128)(2,1)}, bf16[128,1024]{1,0:T(8,128)(2,1)}, u32[]{:S(2)}, u32[]{:S(2)}) collective-permute-start(bf16[128,1024]{1,0:T(8,128)(2,1)} %pad_maximum_fusion.2), channel_id=1, source_target_pairs={{0,5},{1,6},{2,7},{3,0},{4,1},{5,2},{6,3},{7,4},{8,13},{9,14},{10,... | collective-permute-start | bytes 786440 | tf_op jit(solution)/shard_map/ppermute | solution.py:225
  48.0 28.7 %collective-permute-start.2 = (bf16[128,1024]{1,0:T(8,128)(2,1)S(1)}, bf16[128,1024]{1,0:T(8,128)(2,1)}, u32[]{:S(2)}, u32[]{:S(2)}) collective-permute-start(bf16[128,1024]{1,0:T(8,128)(2,1)S(1)} %pad_maximum_fusion.3), channel_id=1, source_target_pairs={{0,4},{1,5},{2,6},{3,7},{4,0},{5,1},{6,2},{7,3},{8,12},{9,13},{10,... | collective-permute-start | bytes 786440 | tf_op jit(solution)/shard_map/ppermute | solution.py:225
  56.2 3.3 %collective-permute-start.9 = (bf16[1024,256]{1,0:T(8,128)(2,1)S(1)}, bf16[1024,256]{1,0:T(8,128)(2,1)}, u32[]{:S(2)}, u32[]{:S(2)}) collective-permute-start(bf16[1024,256]{1,0:T(8,128)(2,1)S(1)} %broadcast_select_fusion), channel_id=1, source_target_pairs={{0,8},{8,0},{16,24},{24,16},{32,40},{40,32},{48,56},{56,48},{64,72... | collective-permute-start | bytes 1572872 | tf_op jit(solution)/shard_map/ppermute | solution.py:212
  57.8 25.1 %collective-permute-start.3 = (bf16[128,1024]{1,0:T(8,128)(2,1)S(1)}, bf16[128,1024]{1,0:T(8,128)(2,1)}, u32[]{:S(2)}, u32[]{:S(2)}) collective-permute-start(bf16[128,1024]{1,0:T(8,128)(2,1)S(1)} %pad_maximum_fusion.4), channel_id=1, source_target_pairs={{0,3},{1,4},{2,5},{3,6},{4,7},{5,0},{6,1},{7,2},{8,11},{9,12},{10,... | collective-permute-start | bytes 786440 | tf_op jit(solution)/shard_map/ppermute | solution.py:225
  99.5 44.7 %copy-start.2 = (f32[1024,256]{1,0:T(8,128)S(1)}, f32[1024,256]{1,0:T(8,128)}, u32[]{:S(2)}) copy-start(f32[1024,256]{1,0:T(8,128)} %get-tuple-element.60) | copy-start | bytes 3145732
  99.5 2.2 %collective-permute-start.10 = (bf16[1024,256]{1,0:T(8,128)(2,1)}, bf16[1024,256]{1,0:T(8,128)(2,1)S(1)}, u32[]{:S(2)}, u32[]{:S(2)}) collective-permute-start(bf16[1024,256]{1,0:T(8,128)(2,1)} %get-tuple-element.42), channel_id=1, source_target_pairs={{0,8},{8,0},{16,24},{24,16},{32,40},{40,32},{48,56},{56,48},{64,72... | collective-permute-start | bytes 1572872 | tf_op jit(solution)/shard_map/ppermute | solution.py:212
  103.1 48.5 %copy-start.13 = (bf16[128,512]{1,0:T(8,128)(2,1)S(1)}, bf16[128,512]{1,0:T(8,128)(2,1)}, u32[]{:S(2)}) copy-start(bf16[128,512]{1,0:T(8,128)(2,1)} %get-tuple-element.57) | copy-start | bytes 393220
  103.2 24.1 %collective-permute-start.18 = (bf16[1024,256]{1,0:T(8,128)(2,1)S(1)}, bf16[1024,256]{1,0:T(8,128)(2,1)S(1)}, u32[]{:S(2)}, u32[]{:S(2)}) collective-permute-start(bf16[1024,256]{1,0:T(8,128)(2,1)S(1)} %get-tuple-element.61), channel_id=1, source_target_pairs={{8,0},{16,8},{24,16},{32,24},{40,32},{48,40},{56,48},{64,56},{72,6... | collective-permute-start | bytes 1572872 | tf_op jit(solution)/shard_map/ppermute | solution.py:208
  105.3 37.3 %collective-permute-start.19 = (bf16[1024,256]{1,0:T(8,128)(2,1)S(1)}, bf16[1024,256]{1,0:T(8,128)(2,1)S(1)}, u32[]{:S(2)}, u32[]{:S(2)}) collective-permute-start(bf16[1024,256]{1,0:T(8,128)(2,1)S(1)} %get-tuple-element.62), channel_id=1, source_target_pairs={{24,0},{32,8},{40,16},{48,24},{56,32},{64,40},{72,48},{80,56},{88,... | collective-permute-start | bytes 1572872 | tf_op jit(solution)/shard_map/ppermute | solution.py:208
  112.8 38.8 %collective-permute-start.11 = (bf16[128,512]{1,0:T(8,128)(2,1)S(1)}, bf16[128,512]{1,0:T(8,128)(2,1)S(1)}, u32[]{:S(2)}, u32[]{:S(2)}) collective-permute-start(bf16[128,512]{1,0:T(8,128)(2,1)S(1)} %copy-done.18), channel_id=1, source_target_pairs={{4,0},{5,1},{6,2},{7,3},{0,4},{1,5},{2,6},{3,7},{12,8},{13,9},{14,... | collective-permute-start | bytes 393224 | tf_op jit(solution)/shard_map/ppermute | solution.py:225
  117.9 36.6 %collective-permute-start.12 = (bf16[128,512]{1,0:T(8,128)(2,1)S(1)}, bf16[128,512]{1,0:T(8,128)(2,1)S(1)}, u32[]{:S(2)}, u32[]{:S(2)}) collective-permute-start(bf16[128,512]{1,0:T(8,128)(2,1)S(1)} %copy-done.17), channel_id=1, source_target_pairs={{5,0},{6,1},{7,2},{0,3},{1,4},{2,5},{3,6},{4,7},{13,8},{14,9},{15,... | collective-permute-start | bytes 393224 | tf_op jit(solution)/shard_map/ppermute | solution.py:225
  118.9 35.8 %collective-permute-start.13 = (bf16[128,512]{1,0:T(8,128)(2,1)S(1)}, bf16[128,512]{1,0:T(8,128)(2,1)S(1)}, u32[]{:S(2)}, u32[]{:S(2)}) collective-permute-start(bf16[128,512]{1,0:T(8,128)(2,1)S(1)} %copy-done.16), channel_id=1, source_target_pairs={{3,0},{4,1},{5,2},{6,3},{7,4},{0,5},{1,6},{2,7},{11,8},{12,9},{13,... | collective-permute-start | bytes 393224 | tf_op jit(solution)/shard_map/ppermute | solution.py:225
  127.3 27.4 %collective-permute-start.14 = (bf16[128,512]{1,0:T(8,128)(2,1)S(1)}, bf16[128,512]{1,0:T(8,128)(2,1)S(1)}, u32[]{:S(2)}, u32[]{:S(2)}) collective-permute-start(bf16[128,512]{1,0:T(8,128)(2,1)S(1)} %copy-done.14), channel_id=1, source_target_pairs={{2,0},{7,1},{4,2},{1,3},{6,4},{3,5},{0,6},{5,7},{10,8},{15,9},{12,... | collective-permute-start | bytes 393224 | tf_op jit(solution)/shard_map/ppermute | solution.py:225
  142.7 12.1 %collective-permute-start.15 = (bf16[128,512]{1,0:T(8,128)(2,1)S(1)}, bf16[128,512]{1,0:T(8,128)(2,1)S(1)}, u32[]{:S(2)}, u32[]{:S(2)}) collective-permute-start(bf16[128,512]{1,0:T(8,128)(2,1)S(1)} %copy-done.15), channel_id=1, source_target_pairs={{6,0},{3,1},{0,2},{5,3},{2,4},{7,5},{4,6},{1,7},{14,8},{11,9},{8,1... | collective-permute-start | bytes 393224 | tf_op jit(solution)/shard_map/ppermute | solution.py:225
  145.1 18.8 %all-to-all-start.1 = ((bf16[8,128,256]{2,1,0:T(8,128)(2,1)}), bf16[8,128,256]{2,1,0:T(8,128)(2,1)S(1)}, u32[]{:S(2)}, u32[]{:S(2)}) async-start(bf16[8,128,256]{2,1,0:T(8,128)(2,1)} %bitcast.12), calls=%async_computation.1 | async-start | bytes 1048576 | tf_op jit(solution)/shard_map/all_to_all | solution.py:243
  151.7 9.6 %collective-permute-start.16 = (bf16[128,512]{1,0:T(8,128)(2,1)S(1)}, bf16[128,512]{1,0:T(8,128)(2,1)S(1)}, u32[]{:S(2)}, u32[]{:S(2)}) collective-permute-start(bf16[128,512]{1,0:T(8,128)(2,1)S(1)} %copy-done.13), channel_id=1, source_target_pairs={{1,0},{2,1},{3,2},{4,3},{5,4},{6,5},{7,6},{0,7},{9,8},{10,9},{11,1... | collective-permute-start | bytes 393224 | tf_op jit(solution)/shard_map/ppermute | solution.py:225
  154.6 7.2 %collective-permute-start.17 = (bf16[128,512]{1,0:T(8,128)(2,1)S(1)}, bf16[128,512]{1,0:T(8,128)(2,1)S(1)}, u32[]{:S(2)}, u32[]{:S(2)}) collective-permute-start(bf16[128,512]{1,0:T(8,128)(2,1)S(1)} %copy-done.12), channel_id=1, source_target_pairs={{7,0},{0,1},{1,2},{2,3},{3,4},{4,5},{5,6},{6,7},{15,8},{8,9},{9,10... | collective-permute-start | bytes 393224 | tf_op jit(solution)/shard_map/ppermute | solution.py:225
  (24 other events, 388.3 us)
